TPU v7x, 1024 devices: a whole 8x8x8 slice. The times are simulated.
1024 devices in a mesh: blk: 64 (over y, z), lev: 16 (over x, core).
Axes of the slice: x: 8, y: 8, z: 8, core: 2. Of those that a mesh axis runs over, the one named last changes fastest.
Arguments:
- io_data: bfloat16 [7, 128, 32768], P(None, 'lev', 'blk'), may hold values from -6 to 6
- io_map: int32 [32768], P('blk'), may hold values from 0 to 32767, as said below
- phys_map: int32 [32768], P('blk'), may hold values from 0 to 32767, as said below
- neighbours: int32 [4, 32768], P(None, 'blk'), may hold values from 0 to 32767, as said below
- column_op: bfloat16 [896, 896], replicated, may hold values from -0.1875 to 0.1875
Outputs:
- tendency: float32 [32768, 7, 128], P(('blk', 'lev'))
Inputs may be any that keep to these rules, and one draw needn't show every extreme that they name: `io_map`: A permutation. The number of positions of block s (positions s * 512 to (s + 1) * 512 - 1) whose image lies in block d depends only on (d - s) modulo the number of blocks, is at most 16, and is exactly 16 for d = s. `phys_map`: A permutation with the same properties as io_map, from element blocks to physics blocks. `neighbours`: each entry is its column's index plus an offset of 1 to 32 in magnitude, modulo 32768; offsets 32 and -32 occur in every block.
All inputs are finite; a program needn't handle non-finite values.
Results may differ from a plain program's by a relative error of at most 0.0029.
Values may be sent and summed in bfloat16 or wider, within the bound.
A program may use at most 32 MiB of HBM per device.

v0:
```python
import jax
import jax.numpy as jnp
from jax import lax
from jax.sharding import PartitionSpec as P

HALO = 32


def padded(cells, sides, width):
    for axis, dim in sides:
        count = lax.axis_size(axis)
        head = lax.slice_in_dim(cells, 0, width, axis=dim)
        tail = lax.slice_in_dim(cells, cells.shape[dim] - width, cells.shape[dim], axis=dim)
        cells = jnp.concatenate(
            [
                lax.ppermute(tail, axis, [(i, (i + 1) % count) for i in range(count)]),
                cells,
                lax.ppermute(head, axis, [((i + 1) % count, i) for i in range(count)]),
            ],
            axis=dim,
        )
    return cells


def pack(values, group, slot, groups, width, capacity):
    onehot = (group[:, None] == jnp.arange(groups, dtype=jnp.int32)[None, :]).astype(jnp.int32)
    ranking = jnp.sum((jnp.cumsum(onehot, axis=0) - 1) * onehot, axis=1)
    where = group * capacity + ranking
    buffer = jnp.zeros((values.shape[0], groups * capacity), values.dtype).at[:, where].set(values)
    slots = jnp.full((groups * capacity,), width, jnp.int32).at[where].set(slot)
    return (buffer.reshape(values.shape[0], groups, capacity), slots.reshape(1, groups, capacity))


def place(arrived, arrived_slots, width):
    rows = arrived.shape[0]
    empty = jnp.zeros((rows, width), arrived.dtype)
    return empty.at[:, arrived_slots.reshape(-1)].set(arrived.reshape(rows, -1), mode="drop")


def local(io_data, io_map, phys_map, neighbours, column_op):
    fields, lev_dev, width = io_data.shape
    rows = fields * lev_dev
    blocks = lax.axis_size("blk")
    here = lax.axis_index("blk")
    capacity = 2 * width // blocks
    total = blocks * width
    flat = io_data.reshape(rows, width)
    io_owner = io_map // width
    io_slot = io_map % width
    buffer, slots = pack(flat, io_owner, io_slot, blocks, width, capacity)
    arrived, arrived_slots = (
        lax.all_to_all(buffer, "blk", split_axis=1, concat_axis=1, tiled=True),
        lax.all_to_all(slots, "blk", split_axis=1, concat_axis=1, tiled=True),
    )
    dynamics = place(arrived, arrived_slots, width).reshape(fields, lev_dev, width)
    extended = padded(dynamics, (("blk", 2),), HALO)
    local_index = (neighbours - here * width + HALO) % total
    values = dynamics.astype(jnp.float32)
    beside_all = jnp.take(extended, local_index[0], axis=2).astype(jnp.float32)
    for index in range(1, 4):
        beside_all = beside_all + jnp.take(extended, local_index[index], axis=2).astype(jnp.float32)
    stepped = (values + 0.2 * (beside_all - 4.0 * values)).astype(jnp.bfloat16).reshape(rows, width)
    phys_owner = phys_map // width
    phys_slot = phys_map % width
    buffer, slots = pack(stepped, phys_owner, phys_slot, blocks, width, capacity)
    landed, landed_slots = (
        lax.all_to_all(buffer, "blk", split_axis=1, concat_axis=1, tiled=True),
        lax.all_to_all(slots, "blk", split_axis=1, concat_axis=1, tiled=True),
    )
    physics = place(landed, landed_slots, width).reshape(fields, lev_dev, width)
    columns = lax.all_to_all(physics, "lev", split_axis=2, concat_axis=1, tiled=True)
    count = columns.shape[2]
    matrix = columns.reshape(fields * columns.shape[1], count)
    result = lax.dot_general(
        matrix, column_op, (((0,), (0,)), ((), ())), preferred_element_type=jnp.float32
    )
    return result.reshape(count, fields, columns.shape[1])


def solution(mesh):
    placed = (P(None, "lev", "blk"), P("blk"), P("blk"), P(None, "blk"), P())
    return jax.shard_map(
        local, mesh=mesh, in_specs=placed, out_specs=P(("blk", "lev"), None, None), check_vma=False
    )
```

profile of v0, /device:TPU:1, one launch (start us, length us, event | category | flops | bytes accessed | tf_op | source)
XLA Modules:
  0.0 141.3 jit_solution(17452506197637459601)
XLA Ops:
  0.0 0.7 add_select_fusion.1
  0.7 1.2 reduce-window.16
  1.9 0.2 slice_reduce_fusion
  2.2 0.1 fusion.1
  2.3 2.4 %scatter_custom_fusion.1 = s32[1024]{0:T(1024)S(1)} fusion(s32[512]{0:T(512)S(1)} %compare_select_fusion.6, s32[512]{0:T(512)S(1)} %get-tuple-element.12, s32[]{:T(128)} %constant.81.clone.1), kind=kCustom, calls=%fused_computation.70 | custom fusion | bytes 4100 | tf_op jit(solution)/shard_map/scatter | solution.py:30
  4.8 0.7 reshape.143
  5.5 24.0 %all-to-all-start.1 = ((s32[1,64,16]{2,0,1:T(1,128)}), s32[1,64,16]{2,0,1:T(1,128)S(1)}, u32[]{:S(2)}, u32[]{:S(2)}) async-start(s32[1,64,16]{2,0,1:T(1,128)} %bitcast.6), calls=%async_computation.1 | async-start | bytes 65536 | tf_op jit(solution)/shard_map/all_to_all | solution.py:53
  29.4 0.7 add_select_fusion
  30.3 0.7 add_select_fusion.3
  31.0 1.2 reduce-window.14
  32.2 0.2 slice_reduce_fusion.1
  32.5 0.1 fusion.3
  32.6 0.1 copy.54
  32.7 1.8 %scatter_custom_fusion.2 = bf16[56,1024]{0,1:T(8,128)(2,1)S(1)} fusion(s32[512]{0:T(512)S(1)} %compare_select_fusion.6, bf16[56,512]{0,1:T(8,128)(2,1)S(1)} %copy.54, bf16[]{:T(256)} %constant.80.clone.1), kind=kCustom, calls=%fused_computation.20 | custom fusion | bytes 245762 | tf_op jit(solution)/shard_map/scatter | solution.py:29
  34.6 1.0 reshape.281
  35.5 4.7 %all-to-all-done.1 = s32[1,64,16]{2,0,1:T(1,128)S(1)} async-done(((s32[1,64,16]{2,0,1:T(1,128)}), s32[1,64,16]{2,0,1:T(1,128)S(1)}, u32[]{:S(2)}, u32[]{:S(2)}) %all-to-all-start.1) | async-done | bytes 4128 | tf_op jit(solution)/shard_map/all_to_all | solution.py:53
  40.2 7.5 %all-to-all-start.2 = ((bf16[64,2,448]{2,1,0:T(2,128)(2,1)}), bf16[64,2,448]{2,1,0:T(2,128)(2,1)S(1)}, u32[]{:S(2)}, u32[]{:S(2)}) async-start(bf16[64,2,448]{2,1,0:T(2,128)(2,1)} %reshape.281), calls=%async_computation.2 | async-start | bytes 262144 | tf_op jit(solution)/shard_map/all_to_all | solution.py:52
  47.7 2.4 %scatter_custom_fusion = s32[1024]{0:T(1024)S(1)} fusion(s32[512]{0:T(512)S(1)} %compare_select_fusion.7, s32[512]{0:T(512)S(1)} %get-tuple-element.14, s32[]{:T(128)} %constant.81.clone.1), kind=kCustom, calls=%fused_computation.72 | custom fusion | bytes 4100 | tf_op jit(solution)/shard_map/scatter | solution.py:30
  50.2 0.7 reshape.140
  50.8 0.5 broadcast.253
  51.3 0.6 reduce.11
  52.0 0.1 reshape.144
  52.1 7.1 %all-to-all-done.2 = bf16[64,2,448]{2,1,0:T(2,128)(2,1)S(1)} async-done(((bf16[64,2,448]{2,1,0:T(2,128)(2,1)}), bf16[64,2,448]{2,1,0:T(2,128)(2,1)S(1)}, u32[]{:S(2)}, u32[]{:S(2)}) %all-to-all-start.2) | async-done | bytes 114720 | tf_op jit(solution)/shard_map/all_to_all | solution.py:52
  59.2 5.1 %all-to-all-start = ((s32[1,64,16]{2,0,1:T(1,128)}), s32[1,64,16]{2,0,1:T(1,128)S(1)}, u32[]{:S(2)}, u32[]{:S(2)}) async-start(s32[1,64,16]{2,0,1:T(1,128)} %bitcast.2), calls=%async_computation | async-start | bytes 65536 | tf_op jit(solution)/shard_map/all_to_all | solution.py:68
  64.3 0.3 reshape.282
  64.5 3.2 %scatter_custom_fusion.3 = bf16[56,512]{0,1:T(8,128)(2,1)S(1)} fusion(s32[1024]{0:T(1024)S(1)} %bitcast.115, bf16[1024,56]{1,0:T(8,128)(2,1)S(1)} %bitcast.102, bf16[]{:T(256)} %constant.80.clone.1), kind=kCustom, calls=%fused_computation.39 | custom fusion | bytes 57346 | tf_op jit(solution)/shard_map/scatter | solution.py:37
  67.7 0.1 copy.55
  67.8 0.1 fusion.26
  67.9 2.9 %collective-permute-start = (bf16[7,8,32]{2,1,0:T(8,128)(2,1)S(1)}, bf16[7,8,32]{2,1,0:T(8,128)(2,1)S(1)}, u32[]{:S(2)}, u32[]{:S(2)}) collective-permute-start(bf16[7,8,32]{2,1,0:T(8,128)(2,1)S(1)} %get-tuple-element.6), channel_id=1, source_target_pairs={{0,16},{16,32},{32,48},{48,64},{64,80},{80,96},{96,112},{112,128},... | collective-permute-start | bytes 10760 | tf_op jit(solution)/shard_map/ppermute | solution.py:16
  70.8 5.9 %collective-permute-start.1 = (bf16[7,8,32]{2,1,0:T(8,128)(2,1)S(1)}, bf16[7,8,32]{2,1,0:T(8,128)(2,1)S(1)}, u32[]{:S(2)}, u32[]{:S(2)}) collective-permute-start(bf16[7,8,32]{2,1,0:T(8,128)(2,1)S(1)} %get-tuple-element.7), channel_id=1, source_target_pairs={{16,0},{32,16},{48,32},{64,48},{80,64},{96,80},{112,96},{128,112},... | collective-permute-start | bytes 10760 | tf_op jit(solution)/shard_map/ppermute | solution.py:18
  76.7 0.0 collective-permute-done
  76.7 0.6 collective-permute-done.1
  77.3 0.1 pad_maximum_fusion
  77.4 0.8 copy.56
  78.2 1.8 %gather_fusion.3 = bf16[512,7,8]{2,1,0:T(8,128)(2,1)S(1)} fusion(bf16[7,8,576]{1,0,2:T(8,128)(2,1)S(1)} %copy.56, s32[1024]{0:T(1024)S(1)} %pad_clamp_fusion), kind=kCustom, calls=%fused_computation.3.clone | custom fusion | bytes 116736 | tf_op jit(solution)/shard_map/jit(_take)/gather | solution.py:61
  80.0 0.7 copy.63
  80.7 1.8 %gather_fusion.2 = bf16[512,7,8]{2,1,0:T(8,128)(2,1)S(1)} fusion(bf16[7,8,576]{1,0,2:T(8,128)(2,1)S(1)} %copy.56, s32[1024]{0:T(1024)S(1)} %pad_clamp_fusion.1), kind=kCustom, calls=%fused_computation.2.clone | custom fusion | bytes 116736 | tf_op jit(solution)/shard_map/jit(_take)/gather | solution.py:61
  82.5 0.7 copy.61
  83.1 1.8 %gather_fusion.1 = bf16[512,7,8]{2,1,0:T(8,128)(2,1)S(1)} fusion(bf16[7,8,576]{1,0,2:T(8,128)(2,1)S(1)} %copy.56, s32[1024]{0:T(1024)S(1)} %pad_clamp_fusion.2), kind=kCustom, calls=%fused_computation.1.clone | custom fusion | bytes 116736 | tf_op jit(solution)/shard_map/jit(_take)/gather | solution.py:61
  85.0 0.7 copy.59
  85.6 1.8 %gather_fusion = bf16[512,7,8]{2,1,0:T(8,128)(2,1)S(1)} fusion(bf16[7,8,576]{1,0,2:T(8,128)(2,1)S(1)} %copy.56, s32[1024]{0:T(1024)S(1)} %pad_clamp_fusion.3), kind=kCustom, calls=%fused_computation.clone | custom fusion | bytes 116736 | tf_op jit(solution)/shard_map/jit(_take)/gather | solution.py:59
  87.4 0.7 copy.57
  88.1 0.1 fusion.18
  88.2 0.1 copy.64
  88.3 1.8 %scatter_custom_fusion.4 = bf16[56,1024]{0,1:T(8,128)(2,1)S(1)} fusion(s32[512]{0:T(512)S(1)} %compare_select_fusion.7, bf16[512,56]{1,0:T(8,128)(2,1)S(1)} %copy.64, bf16[]{:T(256)} %constant.80.clone.1), kind=kCustom, calls=%fused_computation.25 | custom fusion | bytes 114690 | tf_op jit(solution)/shard_map/scatter | solution.py:29
  90.1 1.0 reshape.283
  91.1 0.0 all-to-all-done
  91.1 10.6 %all-to-all-start.3 = ((bf16[64,2,448]{2,1,0:T(2,128)(2,1)}), bf16[64,2,448]{2,1,0:T(2,128)(2,1)S(1)}, u32[]{:S(2)}, u32[]{:S(2)}) async-start(bf16[64,2,448]{2,1,0:T(2,128)(2,1)} %reshape.283), calls=%async_computation.3 | async-start | bytes 262144 | tf_op jit(solution)/shard_map/all_to_all | solution.py:67
  101.7 0.0 copy-start
  101.7 0.8 reduce.10
  102.4 0.1 reshape.141
  102.5 10.6 %all-to-all-done.3 = bf16[64,2,448]{2,1,0:T(2,128)(2,1)S(1)} async-done(((bf16[64,2,448]{2,1,0:T(2,128)(2,1)}), bf16[64,2,448]{2,1,0:T(2,128)(2,1)S(1)}, u32[]{:S(2)}, u32[]{:S(2)}) %all-to-all-start.3) | async-done | bytes 114720 | tf_op jit(solution)/shard_map/all_to_all | solution.py:67
  113.2 0.3 reshape.284
  113.5 3.2 %scatter_custom_fusion.5 = bf16[56,512]{0,1:T(8,128)(2,1)S(1)} fusion(s32[1024]{0:T(1024)S(1)} %bitcast.116, bf16[1024,56]{1,0:T(8,128)(2,1)S(1)} %bitcast.101, bf16[]{:T(256)} %constant.80.clone.1), kind=kCustom, calls=%fused_computation.37 | custom fusion | bytes 57346 | tf_op jit(solution)/shard_map/scatter | solution.py:37
  116.6 0.1 copy.65
  116.7 0.7 copy.66
  117.5 1.4 reshape.285
  118.8 12.1 %all-to-all-start.4 = ((bf16[16,2,896]{2,1,0:T(2,128)(2,1)}), bf16[16,2,896]{2,1,0:T(2,128)(2,1)S(1)}, u32[]{:S(2)}, u32[]{:S(2)}) async-start(bf16[16,2,896]{2,1,0:T(2,128)(2,1)} %reshape.285), calls=%async_computation.4 | async-start | bytes 114688 | tf_op jit(solution)/shard_map/all_to_all | solution.py:71
  130.9 0.0 copy-done
  130.9 1.6 %copy.69 = bf16[896,896]{0,1:T(8,128)(2,1)S(1)} copy(bf16[896,896]{1,0:T(8,128)(2,1)S(1)} %copy-done) | data formatting | bytes 3211264 | tf_op args[4]
  132.5 6.1 %all-to-all-done.4 = bf16[16,2,896]{2,1,0:T(2,128)(2,1)S(1)} async-done(((bf16[16,2,896]{2,1,0:T(2,128)(2,1)}), bf16[16,2,896]{2,1,0:T(2,128)(2,1)S(1)}, u32[]{:S(2)}, u32[]{:S(2)}) %all-to-all-start.4) | async-done | bytes 57376 | tf_op jit(solution)/shard_map/all_to_all | solution.py:71
  138.6 0.8 reshape.286
  139.3 0.7 copy.68
  140.0 1.2 fusion.28
  (23 shorter events, 0.2 us)
Async XLA Ops:
  0.0 32.6 %copy-start.1 = (bf16[7,8,512]{2,1,0:T(8,128)(2,1)S(1)}, bf16[7,8,512]{2,1,0:T(8,128)(2,1)}, u32[]{:S(2)}) copy-start(bf16[7,8,512]{2,1,0:T(8,128)(2,1)} %param.7) | copy-start | bytes 172036
  5.5 34.7 %all-to-all-start.1 = ((s32[1,64,16]{2,0,1:T(1,128)}), s32[1,64,16]{2,0,1:T(1,128)S(1)}, u32[]{:S(2)}, u32[]{:S(2)}) async-start(s32[1,64,16]{2,0,1:T(1,128)} %bitcast.6), calls=%async_computation.1 | async-start | bytes 65536 | tf_op jit(solution)/shard_map/all_to_all | solution.py:53
  40.2 19.0 %all-to-all-start.2 = ((bf16[64,2,448]{2,1,0:T(2,128)(2,1)}), bf16[64,2,448]{2,1,0:T(2,128)(2,1)S(1)}, u32[]{:S(2)}, u32[]{:S(2)}) async-start(bf16[64,2,448]{2,1,0:T(2,128)(2,1)} %reshape.281), calls=%async_computation.2 | async-start | bytes 262144 | tf_op jit(solution)/shard_map/all_to_all | solution.py:52
  59.2 31.9 %all-to-all-start = ((s32[1,64,16]{2,0,1:T(1,128)}), s32[1,64,16]{2,0,1:T(1,128)S(1)}, u32[]{:S(2)}, u32[]{:S(2)}) async-start(s32[1,64,16]{2,0,1:T(1,128)} %bitcast.2), calls=%async_computation | async-start | bytes 65536 | tf_op jit(solution)/shard_map/all_to_all | solution.py:68
  67.9 8.8 %collective-permute-start = (bf16[7,8,32]{2,1,0:T(8,128)(2,1)S(1)}, bf16[7,8,32]{2,1,0:T(8,128)(2,1)S(1)}, u32[]{:S(2)}, u32[]{:S(2)}) collective-permute-start(bf16[7,8,32]{2,1,0:T(8,128)(2,1)S(1)} %get-tuple-element.6), channel_id=1, source_target_pairs={{0,16},{16,32},{32,48},{48,64},{64,80},{80,96},{96,112},{112,128},... | collective-permute-start | bytes 10760 | tf_op jit(solution)/shard_map/ppermute | solution.py:16
  70.8 6.5 %collective-permute-start.1 = (bf16[7,8,32]{2,1,0:T(8,128)(2,1)S(1)}, bf16[7,8,32]{2,1,0:T(8,128)(2,1)S(1)}, u32[]{:S(2)}, u32[]{:S(2)}) collective-permute-start(bf16[7,8,32]{2,1,0:T(8,128)(2,1)S(1)} %get-tuple-element.7), channel_id=1, source_target_pairs={{16,0},{32,16},{48,32},{64,48},{80,64},{96,80},{112,96},{128,112},... | collective-permute-start | bytes 10760 | tf_op jit(solution)/shard_map/ppermute | solution.py:18
  91.1 22.1 %all-to-all-start.3 = ((bf16[64,2,448]{2,1,0:T(2,128)(2,1)}), bf16[64,2,448]{2,1,0:T(2,128)(2,1)S(1)}, u32[]{:S(2)}, u32[]{:S(2)}) async-start(bf16[64,2,448]{2,1,0:T(2,128)(2,1)} %reshape.283), calls=%async_computation.3 | async-start | bytes 262144 | tf_op jit(solution)/shard_map/all_to_all | solution.py:67
  101.7 29.3 %copy-start = (bf16[896,896]{1,0:T(8,128)(2,1)S(1)}, bf16[896,896]{1,0:T(8,128)(2,1)}, u32[]{:S(2)}) copy-start(bf16[896,896]{1,0:T(8,128)(2,1)} %param.11) | copy-start | bytes 4816900
  118.8 19.7 %all-to-all-start.4 = ((bf16[16,2,896]{2,1,0:T(2,128)(2,1)}), bf16[16,2,896]{2,1,0:T(2,128)(2,1)S(1)}, u32[]{:S(2)}, u32[]{:S(2)}) async-start(bf16[16,2,896]{2,1,0:T(2,128)(2,1)} %reshape.285), calls=%async_computation.4 | async-start | bytes 114688 | tf_op jit(solution)/shard_map/all_to_all | solution.py:71
where the time goes:
time: 142 us; the launch traced here: 141 us
  starting transfers between devices  67.9 us (48%)
  local copies, waits for them, and re-layouts  36.1 us (25%)
  waiting for transfers between devices  29.1 us (20%)
  other arithmetic  6.52 us (5%)
    all_to_all x2, starting transfers between devices, local(): lax.all_to_all(slots, 'blk', split_axis=1, concat_axis=1, tiled=True)  29 us
    all_to_all x2, starting transfers between devices, local(): lax.all_to_all(buffer, 'blk', split_axis=1, concat_axis=1, tiled=True)  18 us
    all_to_all x2, waiting for transfers between devices, local(): lax.all_to_all(buffer, 'blk', split_axis=1, concat_axis=1, tiled=True)  17.7 us
    all_to_all x1, starting transfers between devices, local(): lax.all_to_all(physics, 'lev', split_axis=2, concat_axis=1, tiled=True)  12.1 us
    gather x6, local copies, waits for them, and re-layouts, local(): jnp.take(extended, local_index[index], axis=2).astype(jnp.float32)  7.37 us
    scatter x4, local copies, waits for them, and re-layouts, place(): empty.at[:, arrived_slots.reshape(-1)]  6.54 us
    unnamed x11, local copies, waits for them, and re-layouts  6.17 us
    all_to_all x1, waiting for transfers between devices, local(): lax.all_to_all(physics, 'lev', split_axis=2, concat_axis=1, tiled=True)  6.06 us
  transfers between devices with their start and end apart: 7, of which 5 were waited for; matrix products, arithmetic and copies ran while one was open for 21% of the time, Pallas kernels for 0%

commit v1 on v0

v1 whole, which is shorter than its diff:
```python
import functools

import jax
import jax.numpy as jnp
from jax import lax
from jax.experimental import pallas as pl
from jax.experimental.pallas import tpu as pltpu
from jax.sharding import PartitionSpec as P

HALO = 32
CAP = 16
HALF = CAP // 2
LANES = 128
SIDE = LANES // 2
MESH = pl.DeviceIdType.MESH
F32 = jnp.float32
BF16 = jnp.bfloat16
I32 = jnp.int32


def dot_nn(left, right):
    return lax.dot_general(left, right, (((1,), (0,)), ((), ())), preferred_element_type=F32)


def dot_nt(left, right):
    return lax.dot_general(left, right, (((1,), (1,)), ((), ())), preferred_element_type=F32)


def onehot(mask):
    return jnp.where(mask, 1.0, 0.0).astype(BF16)


def rows_of(shape):
    return lax.broadcasted_iota(I32, shape, 0)


def lanes_of(shape):
    return lax.broadcasted_iota(I32, shape, 1)


def both_sides(stack):
    turned = pltpu.roll(stack, SIDE, 1)
    first = lanes_of(stack.shape) < SIDE
    return jnp.where(first, stack, turned).astype(BF16), jnp.where(first, turned, stack).astype(BF16)


def kernel(
    blocks, levs,
    io_hbm, io_map_hbm, phys_map_hbm, near_hbm, op_hbm,
    out_ref,
    io_v, io_map_v, phys_map_v, near_v, op_v, weight,
    pick_lo, pick_hi, step_lo, step_hi, place_lo, place_hi, cells, halo,
    out_a, in_a, out_c, in_c, out_d, in_d, columns,
    load_sem, op_sem, sems, halo_sems,
):
    fields, lev_dev, width = io_v.shape
    rows = blocks * HALF
    total = blocks * width
    shift = width.bit_length() - 1
    me = lax.axis_index("blk")
    my_lev = lax.axis_index("lev")

    loads = [
        pltpu.make_async_copy(src, dst, load_sem.at[at])
        for at, (src, dst) in enumerate(
            ((io_map_hbm, io_map_v), (phys_map_hbm, phys_map_v), (io_hbm, io_v), (near_hbm, near_v))
        )
    ]
    for load in loads:
        load.start()

    barrier = pltpu.get_barrier_semaphore()

    def greet_blk(k, carry):
        pl.semaphore_signal(
            barrier, inc=1, device_id=((me + k) & (blocks - 1), my_lev), device_id_type=MESH
        )
        return carry

    def greet_lev(k, carry):
        pl.semaphore_signal(
            barrier, inc=1, device_id=(me, (my_lev + k) & (levs - 1)), device_id_type=MESH
        )
        return carry

    lax.fori_loop(1, blocks, greet_blk, 0)
    lax.fori_loop(1, levs, greet_lev, 0)

    def load_op(l, carry):
        pltpu.make_async_copy(op_hbm.at[:, l], op_v.at[l, pl.ds(0, fields)], op_sem).start()
        return carry

    lax.fori_loop(0, levs, load_op, 0)

    loads[0].wait()
    loads[1].wait()
    codes = []
    members = []
    for ref in (io_map_v, phys_map_v):
        offset = ((ref[...] >> shift) - me) & (blocks - 1)
        members.append((offset, rows_of((blocks, width)) == offset))
    before = onehot(rows_of((width, width)) < lanes_of((width, width)))
    ranked = dot_nn(
        jnp.concatenate([onehot(members[0][1]), onehot(members[1][1])], axis=0), before
    )
    for at, (offset, member) in enumerate(members):
        part = ranked[at * blocks : (at + 1) * blocks]
        rank = jnp.sum(jnp.where(member, part, 0.0), axis=0, keepdims=True).astype(I32)
        code = offset * HALF + rank
        codes.append(
            (jnp.where(rank < HALF, code, -1), jnp.where(rank >= HALF, code - HALF, -1))
        )

    loads[2].wait()
    meta_row = rows_of((8, width))

    def meta(ref, first):
        slot = (ref[...] & (width - 1)) + 1
        high = (slot >> 5).astype(F32)
        low = (slot & 31).astype(F32)
        return jnp.where(meta_row == first, high, jnp.where(meta_row == first + 1, low, 0.0))

    data = io_v[...].astype(F32).reshape(fields * lev_dev, width)
    one = jnp.concatenate([data, meta(io_map_v, 0)], axis=0)
    own = jnp.concatenate([one, one], axis=0).astype(BF16)
    one = jnp.concatenate([jnp.zeros_like(data), meta(phys_map_v, 2)], axis=0)
    later = jnp.concatenate([one, one], axis=0).astype(BF16)

    where_row = rows_of((rows, width))
    pick_lo[...] = onehot(where_row == codes[1][0])
    pick_hi[...] = onehot(where_row == codes[1][1])
    first_side = lanes_of((rows, LANES)) < SIDE
    lo = dot_nt(onehot(where_row == codes[0][0]), own) + dot_nt(pick_lo[...], later)
    hi = dot_nt(onehot(where_row == codes[0][1]), own) + dot_nt(pick_hi[...], later)
    out_a[...] = jnp.where(first_side, lo, hi).reshape(blocks, HALF, LANES).astype(BF16)

    pl.semaphore_wait(barrier, blocks - 1 + levs - 1)

    def blk_send(src, dst, at):
        def send(k, carry):
            pltpu.make_async_remote_copy(
                src_ref=src.at[k],
                dst_ref=dst.at[k],
                send_sem=sems.at[at],
                recv_sem=sems.at[at + 1],
                device_id=((me + k) & (blocks - 1), my_lev),
                device_id_type=MESH,
            ).start()
            return carry

        lax.fori_loop(1, blocks, send, 0)
        dst[0] = src[0]

    def blk_wait(src, dst, at):
        return pltpu.make_async_remote_copy(
            src_ref=src.at[pl.ds(1, blocks - 1)],
            dst_ref=dst.at[pl.ds(1, blocks - 1)],
            send_sem=sems.at[at],
            recv_sem=sems.at[at + 1],
            device_id=((me + 1) & (blocks - 1), my_lev),
            device_id_type=MESH,
        )

    blk_send(out_a, in_a, 0)

    loads[3].wait()
    near = (near_v[...] - me * width + HALO) & (total - 1)
    near = jnp.where(
        near < HALO, near + width, jnp.where(near < width + HALO, near - HALO, near)
    )
    wide = (width + 2 * HALO, width)
    spot = rows_of(wide)
    taps = jnp.where(spot == lanes_of(wide), 1.0, 0.0)
    for index in range(4):
        taps = taps + jnp.where(spot == near[index : index + 1], 1.0, 0.0)
    taps = taps.astype(BF16)
    step_lo[...] = dot_nt(pick_lo[...], taps).astype(BF16)
    step_hi[...] = dot_nt(pick_hi[...], taps).astype(BF16)

    pltpu.make_async_copy(
        op_v.at[:, pl.ds(0, fields)], op_v.at[:, pl.ds(0, fields)], op_sem
    ).wait()
    depth = SIDE

    def spread(l, carry):
        block = op_v[l].astype(F32)
        block = jnp.where(
            lax.broadcasted_iota(I32, block.shape, 0) < fields, block, 0.0
        ).reshape(depth, block.shape[2])
        weight[pl.ds(pl.multiple_of(l * depth, depth), depth), :] = block.astype(BF16)
        return carry

    lax.fori_loop(0, levs, spread, 0)

    blk_wait(out_a, in_a, 0).wait_recv()
    stack = in_a[...].astype(F32).reshape(rows, LANES)
    choose_row = rows_of((8, LANES))
    choose_lane = lanes_of((8, LANES))
    choose = jnp.zeros((8, LANES), F32)
    for at, lane in enumerate((56, 56 + SIDE, 58, 58 + SIDE)):
        here = choose_row == at
        choose = jnp.where(here & (choose_lane == lane), 32.0, choose)
        choose = jnp.where(here & (choose_lane == lane + 1), 1.0, choose)
    slots = dot_nt(choose.astype(BF16), stack.astype(BF16)).astype(I32)
    left, right = both_sides(stack)
    target = rows_of((width, rows)) + 1
    found = dot_nn(onehot(target == slots[0:1]), left) + dot_nn(onehot(target == slots[1:2]), right)
    cells[...] = found.astype(BF16)

    down = pltpu.make_async_remote_copy(
        src_ref=cells.at[pl.ds(0, HALO)],
        dst_ref=halo.at[pl.ds(HALO, HALO)],
        send_sem=halo_sems.at[0],
        recv_sem=halo_sems.at[1],
        device_id=((me + blocks - 1) & (blocks - 1), my_lev),
        device_id_type=MESH,
    )
    up = pltpu.make_async_remote_copy(
        src_ref=cells.at[pl.ds(width - HALO, HALO)],
        dst_ref=halo.at[pl.ds(0, HALO)],
        send_sem=halo_sems.at[2],
        recv_sem=halo_sems.at[3],
        device_id=((me + 1) & (blocks - 1), my_lev),
        device_id_type=MESH,
    )
    down.start()
    up.start()

    lo = dot_nn(step_lo[:, :width], cells[...])
    hi = dot_nn(step_hi[:, :width], cells[...])
    per = levs * CAP
    line = rows_of((per, rows))
    line = (line >> 4) * (2 * CAP) + (line & (CAP - 1)) + 1
    place_lo[pl.ds(0, per), :] = onehot(line == slots[2:3])
    place_hi[pl.ds(0, per), :] = onehot(line == slots[3:4])
    place_lo[pl.ds(per, per), :] = onehot(line + CAP == slots[2:3])
    place_hi[pl.ds(per, per), :] = onehot(line + CAP == slots[3:4])

    down.wait_recv()
    up.wait_recv()
    lo = lo + dot_nn(step_lo[:, width:], halo[...])
    hi = hi + dot_nn(step_hi[:, width:], halo[...])
    out_c[...] = (0.2 * jnp.where(first_side, lo, hi)).reshape(blocks, HALF, LANES).astype(BF16)
    blk_send(out_c, in_c, 2)

    blk_wait(out_c, in_c, 2).wait_recv()
    left, right = both_sides(in_c[...].astype(F32).reshape(rows, LANES))
    placed = dot_nn(place_lo[...], left) + dot_nn(place_hi[...], right)
    out_d[...] = (
        jnp.where(lanes_of((per, LANES)) < SIDE, placed[:per], placed[per:])
        .reshape(levs, CAP, LANES).astype(BF16)
    )

    def lev_send(k, carry):
        to = (my_lev + k) & (levs - 1)
        pltpu.make_async_remote_copy(
            src_ref=out_d.at[to],
            dst_ref=in_d.at[my_lev],
            send_sem=sems.at[4],
            recv_sem=sems.at[5],
            device_id=(me, to),
            device_id_type=MESH,
        ).start()
        return carry

    lax.fori_loop(1, levs, lev_send, 0)
    in_d[my_lev] = out_d[my_lev]
    lev_wait = pltpu.make_async_remote_copy(
        src_ref=out_d.at[pl.ds(1, levs - 1)],
        dst_ref=in_d.at[pl.ds(1, levs - 1)],
        send_sem=sems.at[4],
        recv_sem=sems.at[5],
        device_id=(me, (my_lev + 1) & (levs - 1)),
        device_id_type=MESH,
    )
    lev_wait.wait_recv()
    side = lanes_of((CAP, LANES)) < SIDE
    for pair in range(levs // 2):
        even = in_d[2 * pair].astype(F32)
        odd = in_d[2 * pair + 1].astype(F32)
        upper = jnp.where(side, even, pltpu.roll(odd, SIDE, 1))
        lower = jnp.where(side, pltpu.roll(even, SIDE, 1), odd)
        columns[:, pair * LANES : (pair + 1) * LANES] = jnp.concatenate(
            [upper, lower], axis=0
        ).astype(BF16)
    result = dot_nn(columns[...], weight[...])
    size = levs * lev_dev
    for field in range(fields):
        out_ref[field] = result[:, field * size : (field + 1) * size]

    blk_wait(out_a, in_a, 0).wait_send()
    down.wait_send()
    up.wait_send()
    blk_wait(out_c, in_c, 2).wait_send()
    lev_wait.wait_send()


def local(io_data, io_map, phys_map, neighbours, column_op):
    fields, lev_dev, width = io_data.shape
    blocks = lax.axis_size("blk")
    levs = lax.axis_size("lev")
    rows = blocks * HALF
    count = width // levs
    span = fields * levs * lev_dev
    any_space = pl.BlockSpec(memory_space=pl.ANY)
    result = pl.pallas_call(
        functools.partial(kernel, blocks, levs),
        out_shape=jax.ShapeDtypeStruct((fields, count, levs * lev_dev), F32),
        in_specs=[any_space] * 5,
        out_specs=pl.BlockSpec(memory_space=pltpu.VMEM),
        scratch_shapes=[
            pltpu.VMEM((fields, lev_dev, width), BF16),
            pltpu.VMEM((1, width), I32),
            pltpu.VMEM((1, width), I32),
            pltpu.VMEM((4, width), I32),
            pltpu.VMEM((levs, fields + 1, lev_dev, span), BF16),
            pltpu.VMEM((levs * SIDE, span), BF16),
            pltpu.VMEM((rows, width), BF16),
            pltpu.VMEM((rows, width), BF16),
            pltpu.VMEM((rows, width + 2 * HALO), BF16),
            pltpu.VMEM((rows, width + 2 * HALO), BF16),
            pltpu.VMEM((width, rows), BF16),
            pltpu.VMEM((width, rows), BF16),
            pltpu.VMEM((width, LANES), BF16),
            pltpu.VMEM((2 * HALO, LANES), BF16),
            pltpu.VMEM((blocks, HALF, LANES), BF16),
            pltpu.VMEM((blocks, HALF, LANES), BF16),
            pltpu.VMEM((blocks, HALF, LANES), BF16),
            pltpu.VMEM((blocks, HALF, LANES), BF16),
            pltpu.VMEM((levs, CAP, LANES), BF16),
            pltpu.VMEM((levs, CAP, LANES), BF16),
            pltpu.VMEM((count, levs * SIDE), BF16),
            pltpu.SemaphoreType.DMA((4,)),
            pltpu.SemaphoreType.DMA,
            pltpu.SemaphoreType.DMA((6,)),
            pltpu.SemaphoreType.DMA((4,)),
        ],
        compiler_params=pltpu.CompilerParams(
            collective_id=0, has_side_effects=True, vmem_limit_bytes=48 * 1024 * 1024
        ),
    )(
        io_data,
        io_map.reshape(1, width),
        phys_map.reshape(1, width),
        neighbours,
        column_op.reshape(fields, levs, lev_dev, span),
    )
    return jnp.transpose(result, (1, 0, 2))


def solution(mesh):
    placed = (P(None, "lev", "blk"), P("blk"), P("blk"), P(None, "blk"), P())
    return jax.shard_map(
        local, mesh=mesh, in_specs=placed, out_specs=P(("blk", "lev"), None, None), check_vma=False
    )
```

time: 142 us -> 59.5 us (0.42)
  starting transfers between devices: 67.9 us -> 0 us
  Pallas kernels: 0 us -> 54.2 us
  local copies, waits for them, and re-layouts: 36.1 us -> 4.94 us
  waiting for transfers between devices: 29.1 us -> 0 us
  other arithmetic: 6.52 us -> 0 us
    all_to_all x5 -> x0, starting transfers between devices: 59.1 us -> none  [the longest x2 29 us: local(): lax.all_to_all(slots, 'blk', split_axis=1, concat_axis=1, tiled=True)]
    pallas_call x0 -> x1, Pallas kernels: none -> 54.2 us  [local(): pl.pallas_call(functools.partial(kernel, blocks, levs), out_shape=jax.Sha...]
    all_to_all x5 -> x0, waiting for transfers between devices: 28.5 us -> none  [the longest x2 17.7 us: local(): lax.all_to_all(buffer, 'blk', split_axis=1, concat_axis=1, tiled=True)]
    scatter x8 -> x0, local copies, waits for them, and re-layouts: 15.1 us -> none  [the longest x4 6.54 us: place(): empty.at[:, arrived_slots.reshape(-1)]]
    gather x8 -> x0, local copies, waits for them, and re-layouts: 9.83 us -> none  [the longest x6 7.37 us: local(): jnp.take(extended, local_index[index], axis=2).astype(jnp.float32)]
    ppermute x2 -> x0, starting transfers between devices: 8.77 us -> none  [the longest x1 5.86 us: padded(): lax.ppermute(head, axis, [((i + 1) % count, i) for i in range(count)])]
    reshape x7 -> x0, local copies, waits for them, and re-layouts: 2.5 us -> none  [the longest x2 1.38 us: pack(): slots.reshape(1, groups, capacity)]
    another operation x4 -> x0, other arithmetic: 2.48 us -> none
  transfers between devices with their start and end apart: 7 -> 0, of which waited for: 5 -> 0; matrix products, arithmetic and copies ran while one was open for 21% -> 0% of each run, Pallas kernels for 0% -> 0%
where the time goes in v1:
time: 59.5 us; the launch traced here: 59.2 us
  Pallas kernels  54.2 us (91%)
  local copies, waits for them, and re-layouts  4.94 us (8%)
    pallas_call x1, Pallas kernels, local(): pl.pallas_call(functools.partial(kernel, blocks, levs), out_shape=jax.Sha...  54.2 us
    unnamed x11, local copies, waits for them, and re-layouts  4.94 us

profile of v1, /device:TPU:1, one launch (start us, length us, event | category | flops | bytes accessed | tf_op | source)
XLA Modules:
  0.0 59.2 jit_solution(2165223895519277651)
XLA Ops:
  0.0 0.0 copy-start
  0.0 1.4 %copy-done = bf16[896,896]{1,0:T(8,128)(2,1)S(1)} copy-done((bf16[896,896]{1,0:T(8,128)(2,1)S(1)}, bf16[896,896]{1,0:T(8,128)(2,1)}, u32[]{:S(2)}) %copy-start) | copy-done | bytes 1605656
  1.4 0.0 copy-start.1
  1.4 0.8 %copy-done.1 = bf16[7,8,512]{2,1,0:T(8,128)(2,1)S(1)} copy-done((bf16[7,8,512]{2,1,0:T(8,128)(2,1)S(1)}, bf16[7,8,512]{2,1,0:T(8,128)(2,1)}, u32[]{:S(2)}) %copy-start.1) | copy-done | bytes 57368
  2.2 0.0 copy-start.2
  2.2 0.7 %copy-done.2 = s32[4,512]{1,0:T(4,128)S(1)} copy-done((s32[4,512]{1,0:T(4,128)S(1)}, s32[4,512]{1,0:T(4,128)}, u32[]{:S(2)}) %copy-start.2) | copy-done | bytes 8216
  2.9 0.0 copy-start.3
  2.9 0.7 %copy-done.3 = s32[512]{0:T(512)S(1)} copy-done((s32[512]{0:T(512)S(1)}, s32[512]{0:T(512)}, u32[]{:S(2)}) %copy-start.3) | copy-done | bytes 2072
  3.6 0.0 copy-start.4
  3.6 0.7 %copy-done.4 = s32[512]{0:T(512)S(1)} copy-done((s32[512]{0:T(512)S(1)}, s32[512]{0:T(512)}, u32[]{:S(2)}) %copy-start.4) | copy-done | bytes 2072
  4.3 54.2 %shard_map.55 = f32[7,32,128]{2,1,0:T(8,128)S(1)} custom-call(bf16[7,8,512]{2,1,0:T(8,128)(2,1)S(1)} %copy-done.1, s32[1,512]{1,0:T(1,128)S(1)} %bitcast.6, s32[1,512]{1,0:T(1,128)S(1)} %bitcast.7, s32[4,512]{1,0:T(4,128)S(1)} %copy-done.2, bf16[7,16,8,896]{3,2,1,0:T(8,128)(2,1)S(1)} %bitcast.4), custom_call_target="tpu_custom_call" | custom-call | tf_op jit(solution)/shard_map/pallas_call | solution.py:306
  58.5 0.6 %copy.7 = f32[32,7,128]{2,0,1:T(8,128)} copy(f32[32,7,128]{2,0,1:T(8,128)S(1)} %bitcast.5) | data formatting | bytes 229376
Async XLA Ops:
  0.0 1.4 %copy-start = (bf16[896,896]{1,0:T(8,128)(2,1)S(1)}, bf16[896,896]{1,0:T(8,128)(2,1)}, u32[]{:S(2)}) copy-start(bf16[896,896]{1,0:T(8,128)(2,1)} %param.9) | copy-start | bytes 4816900
  1.4 0.8 %copy-start.1 = (bf16[7,8,512]{2,1,0:T(8,128)(2,1)S(1)}, bf16[7,8,512]{2,1,0:T(8,128)(2,1)}, u32[]{:S(2)}) copy-start(bf16[7,8,512]{2,1,0:T(8,128)(2,1)} %io_hbm.1) | copy-start | bytes 172036
  2.2 0.7 %copy-start.2 = (s32[4,512]{1,0:T(4,128)S(1)}, s32[4,512]{1,0:T(4,128)}, u32[]{:S(2)}) copy-start(s32[4,512]{1,0:T(4,128)} %near_hbm.1) | copy-start | bytes 24580
  2.9 0.7 %copy-start.3 = (s32[512]{0:T(512)S(1)}, s32[512]{0:T(512)}, u32[]{:S(2)}) copy-start(s32[512]{0:T(512)} %param.6) | copy-start | bytes 6148
  3.6 0.7 %copy-start.4 = (s32[512]{0:T(512)S(1)}, s32[512]{0:T(512)}, u32[]{:S(2)}) copy-start(s32[512]{0:T(512)} %param.7) | copy-start | bytes 6148

commit v2 on v1

v2 whole, which is shorter than its diff:
```python
import functools

import jax
import jax.numpy as jnp
from jax import lax
from jax.experimental import pallas as pl
from jax.experimental.pallas import tpu as pltpu
from jax.sharding import PartitionSpec as P

HALO = 32
CAP = 16
HALF = CAP // 2
LANES = 128
SIDE = LANES // 2
MESH = pl.DeviceIdType.MESH
F32 = jnp.float32
BF16 = jnp.bfloat16
I32 = jnp.int32


def dot_nn(left, right):
    return lax.dot_general(left, right, (((1,), (0,)), ((), ())), preferred_element_type=F32)


def dot_nt(left, right):
    return lax.dot_general(left, right, (((1,), (1,)), ((), ())), preferred_element_type=F32)


def onehot(mask):
    return jnp.where(mask, 1.0, 0.0).astype(BF16)


def rows_of(shape):
    return lax.broadcasted_iota(I32, shape, 0)


def lanes_of(shape):
    return lax.broadcasted_iota(I32, shape, 1)


def both_sides(stack):
    turned = pltpu.roll(stack, SIDE, 1)
    first = lanes_of(stack.shape) < SIDE
    return jnp.where(first, stack, turned).astype(BF16), jnp.where(first, turned, stack).astype(BF16)


def ring(offset, count):
    return min(offset, count - offset)


def kernel(
    blocks, levs,
    io_hbm, io_map_hbm, phys_map_hbm, near_hbm, op_hbm,
    out_ref,
    io_v, io_map_v, phys_map_v, near_v, op_v, weight,
    pick_lo, pick_hi, step_lo, step_hi, step_halo, place_lo, place_hi, cells, halo, partial,
    out_a, in_a, out_c, in_c, out_d, in_d,
    load_sem, op_sem, sems, halo_sems, lev_sems,
):
    fields, lev_dev, width = io_v.shape
    rows = blocks * HALF
    total = blocks * width
    shift = width.bit_length() - 1
    me = lax.axis_index("blk")
    my_lev = lax.axis_index("lev")
    side_z = 1 << ((blocks.bit_length() - 1) // 2)
    side_y = blocks // side_z
    shift_z = side_z.bit_length() - 1
    my_y = me >> shift_z
    my_z = me & (side_z - 1)
    chips = levs // 2
    quarter = side_y // 4
    half_tiles = blocks // 2
    half = half_tiles * HALF
    offsets = sorted(
        ((y, z) for y in range(side_y) for z in range(side_z) if y or z),
        key=lambda at: (-ring(at[0], side_y) - ring(at[1], side_z), at),
    )
    lev_offsets = sorted(
        ((x, core) for x in range(chips) for core in range(2) if x or core),
        key=lambda at: (-ring(at[0], chips), at),
    )
    own_tile = quarter * side_z

    def tile_of(y, z):
        return ((y + quarter) % side_y) * side_z + z

    def at_blk(y, z):
        there = (((my_y + y) & (side_y - 1)) << shift_z) | ((my_z + z) & (side_z - 1))
        return there, my_lev

    def at_lev(x, core):
        return (((my_lev >> 1) + x) & (chips - 1)) * 2 + ((my_lev & 1) ^ core)

    barrier = pltpu.get_barrier_semaphore()
    for y, z in offsets:
        pl.semaphore_signal(barrier, inc=1, device_id=at_blk(y, z), device_id_type=MESH)
    for x, core in lev_offsets:
        pl.semaphore_signal(barrier, inc=1, device_id=(me, at_lev(x, core)), device_id_type=MESH)

    loads = [
        pltpu.make_async_copy(src, dst, load_sem.at[at])
        for at, (src, dst) in enumerate(
            ((io_map_hbm, io_map_v), (phys_map_hbm, phys_map_v), (io_hbm, io_v), (near_hbm, near_v))
        )
    ]
    for load in loads:
        load.start()

    def load_op(l, carry):
        pltpu.make_async_copy(op_hbm.at[:, l], op_v.at[l, pl.ds(0, fields)], op_sem).start()
        return carry

    lax.fori_loop(0, levs, load_op, 0)

    loads[0].wait()
    loads[1].wait()
    codes = []
    members = []
    for ref in (io_map_v, phys_map_v):
        owner = ref[...] >> shift
        to_y = ((owner >> shift_z) - my_y + quarter) & (side_y - 1)
        to_z = ((owner & (side_z - 1)) - my_z) & (side_z - 1)
        tile = (to_y << shift_z) | to_z
        members.append((tile, rows_of((blocks, width)) == tile))
    before = onehot(rows_of((width, width)) < lanes_of((width, width)))
    ranked = dot_nn(
        jnp.concatenate([onehot(members[0][1]), onehot(members[1][1])], axis=0), before
    )
    for at, (tile, member) in enumerate(members):
        part = ranked[at * blocks : (at + 1) * blocks]
        rank = jnp.sum(jnp.where(member, part, 0.0), axis=0, keepdims=True).astype(I32)
        code = tile * HALF + rank
        codes.append(
            (jnp.where(rank < HALF, code, -1), jnp.where(rank >= HALF, code - HALF, -1))
        )

    loads[2].wait()
    meta_row = rows_of((8, width))

    def meta(ref, first):
        slot = (ref[...] & (width - 1)) + 1
        high = (slot >> 5).astype(F32)
        low = (slot & 31).astype(F32)
        return jnp.where(meta_row == first, high, jnp.where(meta_row == first + 1, low, 0.0))

    data = io_v[...].astype(F32).reshape(fields * lev_dev, width)
    one = jnp.concatenate([data, meta(io_map_v, 0)], axis=0)
    own = jnp.concatenate([one, one], axis=0).astype(BF16)
    one = jnp.concatenate([jnp.zeros_like(data), meta(phys_map_v, 2)], axis=0)
    later = jnp.concatenate([one, one], axis=0).astype(BF16)

    where_row = rows_of((rows, width))
    pick_lo[...] = onehot(where_row == codes[1][0])
    pick_hi[...] = onehot(where_row == codes[1][1])
    first_side = lanes_of((rows, LANES)) < SIDE
    lo = dot_nt(onehot(where_row == codes[0][0]), own) + dot_nt(pick_lo[...], later)
    hi = dot_nt(onehot(where_row == codes[0][1]), own) + dot_nt(pick_hi[...], later)
    out_a[...] = jnp.where(first_side, lo, hi).reshape(blocks, HALF, LANES).astype(BF16)

    pl.semaphore_wait(barrier, blocks - 1 + levs - 1)

    def blk_copy(src, dst, at, far, first, count, to):
        return pltpu.make_async_remote_copy(
            src_ref=src.at[pl.ds(first, count)],
            dst_ref=dst.at[pl.ds(first, count)],
            send_sem=sems.at[at],
            recv_sem=sems.at[at + 1 + far],
            device_id=to,
            device_id_type=MESH,
        )

    def blk_send(src, dst, at):
        for y, z in offsets:
            tile = tile_of(y, z)
            blk_copy(src, dst, at, int(tile >= half_tiles), tile, 1, at_blk(y, z)).start()
        dst[own_tile] = src[own_tile]

    def blk_arrived(src, dst, at, far):
        count = half_tiles - 1 + far
        blk_copy(src, dst, at, far, far * half_tiles, count, at_blk(0, 1)).wait_recv()

    def blk_sent(src, dst, at):
        blk_copy(src, dst, at, 0, 0, blocks - 1, at_blk(0, 1)).wait_send()

    blk_send(out_a, in_a, 0)

    loads[3].wait()
    near = (near_v[...] - me * width + HALO) & (total - 1)
    near = jnp.where(
        near < HALO,
        near + width,
        jnp.where((near >= width) & (near < width + HALO), near - width, near),
    )
    wide = (width + 2 * HALO, width)
    spot = rows_of(wide)
    taps = jnp.where(spot == ((lanes_of(wide) + HALO) & (width - 1)), 1.0, 0.0)
    for index in range(4):
        taps = taps + jnp.where(spot == near[index : index + 1], 1.0, 0.0)
    taps = taps.astype(BF16)
    step = dot_nt(pick_lo[...], taps)
    step_lo[...] = step[:, :width].astype(BF16)
    halo_lo = step[:, width:]
    step = dot_nt(pick_hi[...], taps)
    step_hi[...] = step[:, :width].astype(BF16)
    step_halo[...] = jnp.concatenate([halo_lo, step[:, width:]], axis=1).astype(BF16)

    pltpu.make_async_copy(
        op_v.at[:, pl.ds(0, fields)], op_v.at[:, pl.ds(0, fields)], op_sem
    ).wait()
    depth = SIDE

    def spread(l, carry):
        block = op_v[l].astype(F32)
        block = jnp.where(
            lax.broadcasted_iota(I32, block.shape, 0) < fields, block, 0.0
        ).reshape(depth, block.shape[2])
        weight[pl.ds(pl.multiple_of(l * depth, depth), depth), :] = block.astype(BF16)
        return carry

    lax.fori_loop(0, levs, spread, 0)

    choose_row = rows_of((8, LANES))
    choose_lane = lanes_of((8, LANES))
    choose = jnp.zeros((8, LANES), F32)
    for at, lane in enumerate((56, 56 + SIDE, 58, 58 + SIDE)):
        here = choose_row == at
        choose = jnp.where(here & (choose_lane == lane), 32.0, choose)
        choose = jnp.where(here & (choose_lane == lane + 1), 1.0, choose)
    choose = choose.astype(BF16)

    def opened(buffer, far):
        stack = buffer[pl.ds(far * half_tiles, half_tiles)].astype(F32).reshape(half, LANES)
        return stack, both_sides(stack)

    slots = []
    edge = 2 * HALO

    def found(first, count, at, sides):
        target = ((rows_of((count, half)) + (first + width - HALO)) & (width - 1)) + 1
        return dot_nn(onehot(target == at[0:1]), sides[0]) + dot_nn(
            onehot(target == at[1:2]), sides[1]
        )

    blk_arrived(out_a, in_a, 0, 0)
    stack, sides = opened(in_a, 0)
    slots.append(dot_nt(choose, stack.astype(BF16)).astype(I32))
    partial[...] = found(0, width, slots[0], sides)

    blk_arrived(out_a, in_a, 0, 1)
    stack, sides = opened(in_a, 1)
    slots.append(dot_nt(choose, stack.astype(BF16)).astype(I32))
    cells[pl.ds(0, edge), :] = (partial[pl.ds(0, edge), :] + found(0, edge, slots[1], sides)).astype(BF16)

    up = pltpu.make_async_remote_copy(
        src_ref=cells.at[pl.ds(0, HALO)],
        dst_ref=halo.at[pl.ds(0, HALO)],
        send_sem=halo_sems.at[0],
        recv_sem=halo_sems.at[1],
        device_id=((me + 1) & (blocks - 1), my_lev),
        device_id_type=MESH,
    )
    down = pltpu.make_async_remote_copy(
        src_ref=cells.at[pl.ds(HALO, HALO)],
        dst_ref=halo.at[pl.ds(HALO, HALO)],
        send_sem=halo_sems.at[2],
        recv_sem=halo_sems.at[3],
        device_id=((me + blocks - 1) & (blocks - 1), my_lev),
        device_id_type=MESH,
    )
    up.start()
    down.start()

    if width > edge:
        rest = width - edge
        cells[pl.ds(edge, rest), :] = (
            partial[pl.ds(edge, rest), :] + found(edge, rest, slots[1], sides)
        ).astype(BF16)
    lo = dot_nn(step_lo[...], cells[...])
    hi = dot_nn(step_hi[...], cells[...])
    partial[...] = jnp.where(first_side, lo, hi)

    up.wait_recv()
    down.wait_recv()
    beside = halo[...]
    on_side = lanes_of(beside.shape) < SIDE
    none = jnp.zeros_like(beside)
    beside = jnp.concatenate(
        [jnp.where(on_side, beside, none), jnp.where(on_side, none, beside)], axis=0
    )
    summed = partial[...] + dot_nn(step_halo[...], beside)
    out_c[...] = (0.2 * summed).reshape(blocks, HALF, LANES).astype(BF16)
    blk_send(out_c, in_c, 3)

    per = levs * CAP
    line = rows_of((per, half))
    line = (line >> 4) * (2 * CAP) + (line & (CAP - 1)) + 1
    for far in range(2):
        span = slice(far * half, (far + 1) * half)
        place_lo[0:per, span] = onehot(line == slots[far][2:3])
        place_hi[0:per, span] = onehot(line == slots[far][3:4])
        place_lo[per : 2 * per, span] = onehot(line + CAP == slots[far][2:3])
        place_hi[per : 2 * per, span] = onehot(line + CAP == slots[far][3:4])

    blk_arrived(out_c, in_c, 3, 0)
    _, sides = opened(in_c, 0)
    partial[...] = dot_nn(place_lo[:, :half], sides[0]) + dot_nn(place_hi[:, :half], sides[1])
    blk_arrived(out_c, in_c, 3, 1)
    _, sides = opened(in_c, 1)
    placed = partial[...] + (
        dot_nn(place_lo[:, half:], sides[0]) + dot_nn(place_hi[:, half:], sides[1])
    )
    out_d[...] = (
        jnp.where(lanes_of((per, LANES)) < SIDE, placed[:per], placed[per:])
        .reshape(levs, CAP, LANES).astype(BF16)
    )

    for x, core in lev_offsets:
        to = at_lev(x, core)
        pltpu.make_async_remote_copy(
            src_ref=out_d.at[to],
            dst_ref=in_d.at[my_lev],
            send_sem=sems.at[6],
            recv_sem=lev_sems.at[x],
            device_id=(me, to),
            device_id_type=MESH,
        ).start()
    in_d[my_lev] = out_d[my_lev]

    def lev_wait(x, count):
        return pltpu.make_async_remote_copy(
            src_ref=out_d.at[pl.ds(0, count)],
            dst_ref=in_d.at[pl.ds(0, count)],
            send_sem=sems.at[6],
            recv_sem=lev_sems.at[x],
            device_id=(me, at_lev(0, 1)),
            device_id_type=MESH,
        )

    side = lanes_of((CAP, LANES)) < SIDE
    result = None
    for x in sorted(range(chips), key=lambda at: ring(at, chips)):
        lev_wait(x, 2 if x else 1).wait_recv()
        chip = ((my_lev >> 1) - x) & (chips - 1)
        even = in_d[2 * chip].astype(F32)
        odd = in_d[2 * chip + 1].astype(F32)
        upper = jnp.where(side, even, pltpu.roll(odd, SIDE, 1))
        lower = jnp.where(side, pltpu.roll(even, SIDE, 1), odd)
        columns = jnp.concatenate([upper, lower], axis=0).astype(BF16)
        term = dot_nn(columns, weight[pl.ds(pl.multiple_of(chip * LANES, LANES), LANES), :])
        result = term if result is None else result + term
    size = levs * lev_dev
    for field in range(fields):
        out_ref[field] = result[:, field * size : (field + 1) * size]

    blk_sent(out_a, in_a, 0)
    up.wait_send()
    down.wait_send()
    blk_sent(out_c, in_c, 3)
    lev_wait(0, levs - 1).wait_send()


def local(io_data, io_map, phys_map, neighbours, column_op):
    fields, lev_dev, width = io_data.shape
    blocks = lax.axis_size("blk")
    levs = lax.axis_size("lev")
    rows = blocks * HALF
    count = width // levs
    span = fields * levs * lev_dev
    any_space = pl.BlockSpec(memory_space=pl.ANY)
    result = pl.pallas_call(
        functools.partial(kernel, blocks, levs),
        out_shape=jax.ShapeDtypeStruct((fields, count, levs * lev_dev), F32),
        in_specs=[any_space] * 5,
        out_specs=pl.BlockSpec(memory_space=pltpu.VMEM),
        scratch_shapes=[
            pltpu.VMEM((fields, lev_dev, width), BF16),
            pltpu.VMEM((1, width), I32),
            pltpu.VMEM((1, width), I32),
            pltpu.VMEM((4, width), I32),
            pltpu.VMEM((levs, fields + 1, lev_dev, span), BF16),
            pltpu.VMEM((levs * SIDE, span), BF16),
            pltpu.VMEM((rows, width), BF16),
            pltpu.VMEM((rows, width), BF16),
            pltpu.VMEM((rows, width), BF16),
            pltpu.VMEM((rows, width), BF16),
            pltpu.VMEM((rows, 4 * HALO), BF16),
            pltpu.VMEM((width, rows), BF16),
            pltpu.VMEM((width, rows), BF16),
            pltpu.VMEM((width, LANES), BF16),
            pltpu.VMEM((2 * HALO, LANES), BF16),
            pltpu.VMEM((width, LANES), F32),
            pltpu.VMEM((blocks, HALF, LANES), BF16),
            pltpu.VMEM((blocks, HALF, LANES), BF16),
            pltpu.VMEM((blocks, HALF, LANES), BF16),
            pltpu.VMEM((blocks, HALF, LANES), BF16),
            pltpu.VMEM((levs, CAP, LANES), BF16),
            pltpu.VMEM((levs, CAP, LANES), BF16),
            pltpu.SemaphoreType.DMA((4,)),
            pltpu.SemaphoreType.DMA,
            pltpu.SemaphoreType.DMA((7,)),
            pltpu.SemaphoreType.DMA((4,)),
            pltpu.SemaphoreType.DMA((levs // 2,)),
        ],
        compiler_params=pltpu.CompilerParams(
            collective_id=0, has_side_effects=True, vmem_limit_bytes=60 * 1024 * 1024
        ),
    )(
        io_data,
        io_map.reshape(1, width),
        phys_map.reshape(1, width),
        neighbours,
        column_op.reshape(fields, levs, lev_dev, span),
    )
    return jnp.transpose(result, (1, 0, 2))


def solution(mesh):
    placed = (P(None, "lev", "blk"), P("blk"), P("blk"), P(None, "blk"), P())
    return jax.shard_map(
        local, mesh=mesh, in_specs=placed, out_specs=P(("blk", "lev"), None, None), check_vma=False
    )
```

time: 59.5 us -> 51.6 us (0.87)
  Pallas kernels: 54.2 us -> 49.8 us
  local copies, waits for them, and re-layouts: 4.94 us -> 1.55 us
    pallas_call x1, Pallas kernels: 54.2 us -> 49.8 us  [local(): pl.pallas_call(functools.partial(kernel, blocks, levs), out_shape=jax.Sha...]
    unnamed x11 -> x1, local copies, waits for them, and re-layouts: 4.94 us -> 1.55 us
where the time goes in v2:
time: 51.6 us; the launch traced here: 51.4 us
  Pallas kernels  49.8 us (97%)
  local copies, waits for them, and re-layouts  1.55 us (3%)
    pallas_call x1, Pallas kernels, local(): pl.pallas_call(functools.partial(kernel, blocks, levs), out_shape=jax.Sha...  49.8 us
    unnamed x1, local copies, waits for them, and re-layouts  1.55 us

profile of v2, /device:TPU:1, one launch (start us, length us, event | category | flops | bytes accessed | tf_op | source)
XLA Modules:
  0.0 51.4 jit_solution(915027440709357926)
XLA Ops:
  0.0 49.8 %shard_map.55 = f32[7,32,128]{2,1,0:T(8,128)} custom-call(bf16[7,8,512]{2,1,0:T(8,128)(2,1)} %io_hbm.1, s32[1,512]{1,0:T(1,128)} %bitcast.6, s32[1,512]{1,0:T(1,128)} %bitcast.7, s32[4,512]{1,0:T(4,128)} %near_hbm.1, bf16[7,16,8,896]{3,2,1,0:T(8,128)(2,1)} %bitcast.4), custom_call_target="tpu_custom_call" | custom-call | tf_op jit(solution)/shard_map/pallas_call | solution.py:371
  49.8 1.6 %copy.7 = f32[32,7,128]{2,0,1:T(8,128)} copy(f32[32,7,128]{2,0,1:T(8,128)} %bitcast.5) | data formatting | bytes 229376

commit v3 on v2

--- a/solution.py
+++ b/solution.py
@@ -54,8 +54,8 @@
     out_ref,
     io_v, io_map_v, phys_map_v, near_v, op_v, weight,
     pick_lo, pick_hi, step_lo, step_hi, step_halo, place_lo, place_hi, cells, halo, partial,
-    out_a, in_a, out_c, in_c, out_d, in_d,
-    load_sem, op_sem, sems, halo_sems, lev_sems,
+    out_a, mid_a, in_a, out_c, in_c, out_d, in_d,
+    load_sem, op_sem, sems, row_sems, halo_sems, lev_sems, row_hello, column_hello, lev_hello,
 ):
     fields, lev_dev, width = io_v.shape
     rows = blocks * HALF
@@ -92,11 +92,21 @@
     def at_lev(x, core):
         return (((my_lev >> 1) + x) & (chips - 1)) * 2 + ((my_lev & 1) ^ core)
 
-    barrier = pltpu.get_barrier_semaphore()
-    for y, z in offsets:
-        pl.semaphore_signal(barrier, inc=1, device_id=at_blk(y, z), device_id_type=MESH)
-    for x, core in lev_offsets:
-        pl.semaphore_signal(barrier, inc=1, device_id=(me, at_lev(x, core)), device_id_type=MESH)
+    def turn(at, count):
+        return jnp.where(at < count // 2, at, count // 2 + count - 1 - at)
+
+    row_turn = turn(my_y, side_y)
+    lev_turn = turn(my_lev >> 1, chips) * 2 + (my_lev & 1)
+
+    def turn_at_row(y):
+        return turn((my_y + y) & (side_y - 1), side_y)
+
+    def turn_at_lev(x, core):
+        there = at_lev(x, core)
+        return turn(there >> 1, chips) * 2 + (there & 1)
+
+    far_rows = sorted(range(1, side_y), key=lambda at: -ring(at, side_y))
+    far_columns = sorted(range(1, side_z), key=lambda at: -ring(at, side_z))
 
     loads = [
         pltpu.make_async_copy(src, dst, load_sem.at[at])
@@ -107,12 +117,44 @@
     for load in loads:
         load.start()
 
+    barrier = pltpu.get_barrier_semaphore()
+
+    def greet(to, semaphore=barrier):
+        pl.semaphore_signal(semaphore, inc=1, device_id=to, device_id_type=MESH)
+
+    for y in far_rows:
+        pl.when(turn_at_row(y) > row_turn)(functools.partial(greet, at_blk(y, 0)))
+    for x, core in lev_offsets:
+        pl.when(turn_at_lev(x, core) > lev_turn)(
+            functools.partial(greet, (me, at_lev(x, core)))
+        )
+    for z in range(1, side_z):
+
+        @pl.when(my_z + z < side_z)
+        def _():
+            for y in far_rows + [0]:
+                greet(at_blk(y, z))
+
+    def hear(semaphore, count):
+        pl.when(count > 0)(functools.partial(pl.semaphore_wait, semaphore, count))
+
+    hear(barrier, my_z * side_y + row_turn + lev_turn)
+    for z in range(1, side_z):
+        pl.when(my_z >= z)(functools.partial(greet, at_blk(0, -z), column_hello.at[z - 1]))
+    for y in far_rows:
+        pl.when(turn_at_row(y) < row_turn)(functools.partial(greet, at_blk(y, 0), row_hello))
+    for x, core in lev_offsets:
+        pl.when(turn_at_lev(x, core) < lev_turn)(
+            functools.partial(greet, (me, at_lev(x, core)), lev_hello)
+        )
+
     def load_op(l, carry):
         pltpu.make_async_copy(op_hbm.at[:, l], op_v.at[l, pl.ds(0, fields)], op_sem).start()
         return carry
 
     lax.fori_loop(0, levs, load_op, 0)
 
+    before = onehot(rows_of((width, width)) < lanes_of((width, width)))
     loads[0].wait()
     loads[1].wait()
     codes = []
@@ -123,7 +165,6 @@
         to_z = ((owner & (side_z - 1)) - my_z) & (side_z - 1)
         tile = (to_y << shift_z) | to_z
         members.append((tile, rows_of((blocks, width)) == tile))
-    before = onehot(rows_of((width, width)) < lanes_of((width, width)))
     ranked = dot_nn(
         jnp.concatenate([onehot(members[0][1]), onehot(members[1][1])], axis=0), before
     )
@@ -150,15 +191,64 @@
     one = jnp.concatenate([jnp.zeros_like(data), meta(phys_map_v, 2)], axis=0)
     later = jnp.concatenate([one, one], axis=0).astype(BF16)
 
-    where_row = rows_of((rows, width))
-    pick_lo[...] = onehot(where_row == codes[1][0])
-    pick_hi[...] = onehot(where_row == codes[1][1])
+    def slot_of(y):
+        return (y + quarter) % side_y
+
+    def tile_copy(y, z):
+        return pltpu.make_async_remote_copy(
+            src_ref=out_a.at[slot_of(y), z],
+            dst_ref=in_a.at[slot_of(y), z],
+            send_sem=sems.at[0 if z else 7],
+            recv_sem=sems.at[1 if z else 8],
+            device_id=at_blk(y, z),
+            device_id_type=MESH,
+        )
+
     first_side = lanes_of((rows, LANES)) < SIDE
-    lo = dot_nt(onehot(where_row == codes[0][0]), own) + dot_nt(pick_lo[...], later)
-    hi = dot_nt(onehot(where_row == codes[0][1]), own) + dot_nt(pick_hi[...], later)
-    out_a[...] = jnp.where(first_side, lo, hi).reshape(blocks, HALF, LANES).astype(BF16)
-
-    pl.semaphore_wait(barrier, blocks - 1 + levs - 1)
+    for far in (1, 0):
+        where_row = rows_of((half, width)) + far * half
+        here = pl.ds(far * half, half)
+        pick_lo[here, :] = onehot(where_row == codes[1][0])
+        pick_hi[here, :] = onehot(where_row == codes[1][1])
+        lo = dot_nt(onehot(where_row == codes[0][0]), own) + dot_nt(pick_lo[here, :], later)
+        hi = dot_nt(onehot(where_row == codes[0][1]), own) + dot_nt(pick_hi[here, :], later)
+        out_a[pl.ds(far * (side_y // 2), side_y // 2)] = (
+            jnp.where(first_side[:half], lo, hi)
+            .reshape(side_y // 2, side_z, HALF, LANES).astype(BF16)
+        )
+        for z in far_columns:
+
+            @pl.when(my_z + z >= side_z)
+            def _():
+                for y in far_rows + [0]:
+                    if slot_of(y) // (side_y // 2) == far:
+                        tile_copy(y, z).start()
+
+    for y in far_rows:
+        pl.when(turn_at_row(y) < row_turn)(tile_copy(y, 0).start)
+    hear(row_hello, side_y - 1 - row_turn)
+    for y in far_rows:
+        pl.when(turn_at_row(y) > row_turn)(tile_copy(y, 0).start)
+
+    def row_copy(first, count, z, to):
+        return pltpu.make_async_remote_copy(
+            src_ref=out_a.at[pl.ds(first, count), z],
+            dst_ref=mid_a.at[pl.ds(first, count), z],
+            send_sem=row_sems.at[z - 1, 0],
+            recv_sem=row_sems.at[z - 1, 1],
+            device_id=to,
+            device_id_type=MESH,
+        )
+
+    for z in range(1, side_z):
+
+        @pl.when(my_z + z < side_z)
+        def _():
+            for y in far_rows:
+                row_copy(slot_of(y), 1, z, at_blk(y, 0)).start()
+
+    mid_a[quarter] = out_a[quarter]
+    in_a[quarter, 0] = out_a[quarter, 0]
 
     def blk_copy(src, dst, at, far, first, count, to):
         return pltpu.make_async_remote_copy(
@@ -182,8 +272,6 @@
 
     def blk_sent(src, dst, at):
         blk_copy(src, dst, at, 0, 0, blocks - 1, at_blk(0, 1)).wait_send()
-
-    blk_send(out_a, in_a, 0)
 
     loads[3].wait()
     near = (near_v[...] - me * width + HALO) & (total - 1)
@@ -229,28 +317,48 @@
         choose = jnp.where(here & (choose_lane == lane + 1), 1.0, choose)
     choose = choose.astype(BF16)
 
-    def opened(buffer, far):
-        stack = buffer[pl.ds(far * half_tiles, half_tiles)].astype(F32).reshape(half, LANES)
-        return stack, both_sides(stack)
-
-    slots = []
+    def column_copy(first, count, z):
+        return pltpu.make_async_remote_copy(
+            src_ref=mid_a.at[:, pl.ds(first, count)],
+            dst_ref=in_a.at[:, pl.ds(first, count)],
+            send_sem=sems.at[0],
+            recv_sem=sems.at[1],
+            device_id=at_blk(0, z),
+            device_id_type=MESH,
+        )
+
+    for z in range(1, side_z):
+
+        @pl.when(my_z + z < side_z)
+        def _():
+            row_copy(0, side_y - 1, z, at_blk(1, 0)).wait_recv()
+            pl.semaphore_wait(column_hello.at[z - 1], 1)
+            column_copy(z, 1, z).start()
+
+    row_tiles = pltpu.make_async_remote_copy(
+        src_ref=out_a.at[pl.ds(0, side_y - 1), 0],
+        dst_ref=in_a.at[pl.ds(0, side_y - 1), 0],
+        send_sem=sems.at[7],
+        recv_sem=sems.at[8],
+        device_id=at_blk(1, 0),
+        device_id_type=MESH,
+    )
+
     edge = 2 * HALO
-
-    def found(first, count, at, sides):
-        target = ((rows_of((count, half)) + (first + width - HALO)) & (width - 1)) + 1
-        return dot_nn(onehot(target == at[0:1]), sides[0]) + dot_nn(
-            onehot(target == at[1:2]), sides[1]
-        )
-
-    blk_arrived(out_a, in_a, 0, 0)
-    stack, sides = opened(in_a, 0)
-    slots.append(dot_nt(choose, stack.astype(BF16)).astype(I32))
-    partial[...] = found(0, width, slots[0], sides)
-
-    blk_arrived(out_a, in_a, 0, 1)
-    stack, sides = opened(in_a, 1)
-    slots.append(dot_nt(choose, stack.astype(BF16)).astype(I32))
-    cells[pl.ds(0, edge), :] = (partial[pl.ds(0, edge), :] + found(0, edge, slots[1], sides)).astype(BF16)
+    row_tiles.wait_recv()
+    column_copy(1, side_z - 1, 1).wait_recv()
+    stack = in_a[...].astype(F32).reshape(rows, LANES)
+    sides = both_sides(stack)
+    slots = dot_nt(choose, stack.astype(BF16)).astype(I32)
+
+    def found(first, count):
+        target = ((rows_of((count, rows)) + (first + width - HALO)) & (width - 1)) + 1
+        return (
+            dot_nn(onehot(target == slots[0:1]), sides[0])
+            + dot_nn(onehot(target == slots[1:2]), sides[1])
+        ).astype(BF16)
+
+    cells[pl.ds(0, edge), :] = found(0, edge)
 
     up = pltpu.make_async_remote_copy(
         src_ref=cells.at[pl.ds(0, HALO)],
@@ -273,9 +381,7 @@
 
     if width > edge:
         rest = width - edge
-        cells[pl.ds(edge, rest), :] = (
-            partial[pl.ds(edge, rest), :] + found(edge, rest, slots[1], sides)
-        ).astype(BF16)
+        cells[pl.ds(edge, rest), :] = found(edge, rest)
     lo = dot_nn(step_lo[...], cells[...])
     hi = dot_nn(step_hi[...], cells[...])
     partial[...] = jnp.where(first_side, lo, hi)
@@ -293,20 +399,22 @@
     blk_send(out_c, in_c, 3)
 
     per = levs * CAP
-    line = rows_of((per, half))
+    line = rows_of((per, rows))
     line = (line >> 4) * (2 * CAP) + (line & (CAP - 1)) + 1
-    for far in range(2):
-        span = slice(far * half, (far + 1) * half)
-        place_lo[0:per, span] = onehot(line == slots[far][2:3])
-        place_hi[0:per, span] = onehot(line == slots[far][3:4])
-        place_lo[per : 2 * per, span] = onehot(line + CAP == slots[far][2:3])
-        place_hi[per : 2 * per, span] = onehot(line + CAP == slots[far][3:4])
+    place_lo[0:per, :] = onehot(line == slots[2:3])
+    place_hi[0:per, :] = onehot(line == slots[3:4])
+    place_lo[per : 2 * per, :] = onehot(line + CAP == slots[2:3])
+    place_hi[per : 2 * per, :] = onehot(line + CAP == slots[3:4])
+
+    def opened(buffer, far):
+        stack = buffer[pl.ds(far * half_tiles, half_tiles)].astype(F32).reshape(half, LANES)
+        return both_sides(stack)
 
     blk_arrived(out_c, in_c, 3, 0)
-    _, sides = opened(in_c, 0)
+    sides = opened(in_c, 0)
     partial[...] = dot_nn(place_lo[:, :half], sides[0]) + dot_nn(place_hi[:, :half], sides[1])
     blk_arrived(out_c, in_c, 3, 1)
-    _, sides = opened(in_c, 1)
+    sides = opened(in_c, 1)
     placed = partial[...] + (
         dot_nn(place_lo[:, half:], sides[0]) + dot_nn(place_hi[:, half:], sides[1])
     )
@@ -315,6 +423,7 @@
         .reshape(levs, CAP, LANES).astype(BF16)
     )
 
+    hear(lev_hello, levs - 1 - lev_turn)
     for x, core in lev_offsets:
         to = at_lev(x, core)
         pltpu.make_async_remote_copy(
@@ -353,7 +462,10 @@
     for field in range(fields):
         out_ref[field] = result[:, field * size : (field + 1) * size]
 
-    blk_sent(out_a, in_a, 0)
+    row_tiles.wait_send()
+    column_copy(1, side_z - 1, 1).wait_send()
+    for z in range(1, side_z):
+        pl.when(my_z + z < side_z)(row_copy(0, side_y - 1, z, at_blk(1, 0)).wait_send)
     up.wait_send()
     down.wait_send()
     blk_sent(out_c, in_c, 3)
@@ -367,6 +479,8 @@
     rows = blocks * HALF
     count = width // levs
     span = fields * levs * lev_dev
+    side_z = 1 << ((blocks.bit_length() - 1) // 2)
+    side_y = blocks // side_z
     any_space = pl.BlockSpec(memory_space=pl.ANY)
     result = pl.pallas_call(
         functools.partial(kernel, blocks, levs),
@@ -390,17 +504,22 @@
             pltpu.VMEM((width, LANES), BF16),
             pltpu.VMEM((2 * HALO, LANES), BF16),
             pltpu.VMEM((width, LANES), F32),
-            pltpu.VMEM((blocks, HALF, LANES), BF16),
-            pltpu.VMEM((blocks, HALF, LANES), BF16),
+            pltpu.VMEM((side_y, side_z, HALF, LANES), BF16),
+            pltpu.VMEM((side_y, side_z, HALF, LANES), BF16),
+            pltpu.VMEM((side_y, side_z, HALF, LANES), BF16),
             pltpu.VMEM((blocks, HALF, LANES), BF16),
             pltpu.VMEM((blocks, HALF, LANES), BF16),
             pltpu.VMEM((levs, CAP, LANES), BF16),
             pltpu.VMEM((levs, CAP, LANES), BF16),
             pltpu.SemaphoreType.DMA((4,)),
             pltpu.SemaphoreType.DMA,
-            pltpu.SemaphoreType.DMA((7,)),
+            pltpu.SemaphoreType.DMA((9,)),
+            pltpu.SemaphoreType.DMA((side_z - 1, 2)),
             pltpu.SemaphoreType.DMA((4,)),
             pltpu.SemaphoreType.DMA((levs // 2,)),
+            pltpu.SemaphoreType.REGULAR,
+            pltpu.SemaphoreType.REGULAR((side_z - 1,)),
+            pltpu.SemaphoreType.REGULAR,
         ],
         compiler_params=pltpu.CompilerParams(
             collective_id=0, has_side_effects=True, vmem_limit_bytes=60 * 1024 * 1024

time: 51.6 us -> 50.9 us (0.986)
  Pallas kernels: 49.8 us -> 49.1 us
    pallas_call x1, Pallas kernels: 49.8 us -> 49.1 us  [local(): pl.pallas_call(functools.partial(kernel, blocks, levs), out_shape=jax.Sha...]
where the time goes in v3:
time: 50.9 us; the launch traced here: 50.7 us
  Pallas kernels  49.1 us (96%)
  local copies, waits for them, and re-layouts  1.55 us (3%)
    pallas_call x1, Pallas kernels, local(): pl.pallas_call(functools.partial(kernel, blocks, levs), out_shape=jax.Sha...  49.1 us
    unnamed x1, local copies, waits for them, and re-layouts  1.55 us

profile of v3, /device:TPU:1, one launch (start us, length us, event | category | flops | bytes accessed | tf_op | source)
XLA Modules:
  0.0 50.7 jit_solution(6928372340532411244)
XLA Ops:
  0.0 49.1 %shard_map.55 = f32[7,32,128]{2,1,0:T(8,128)} custom-call(bf16[7,8,512]{2,1,0:T(8,128)(2,1)} %io_hbm.1, s32[1,512]{1,0:T(1,128)} %bitcast.6, s32[1,512]{1,0:T(1,128)} %bitcast.7, s32[4,512]{1,0:T(4,128)} %near_hbm.1, bf16[7,16,8,896]{3,2,1,0:T(8,128)(2,1)} %bitcast.4), custom_call_target="tpu_custom_call" | custom-call | tf_op jit(solution)/shard_map/pallas_call | solution.py:485
  49.1 1.6 %copy.7 = f32[32,7,128]{2,0,1:T(8,128)} copy(f32[32,7,128]{2,0,1:T(8,128)} %bitcast.5) | data formatting | bytes 229376

commit v4 on v3

--- a/solution.py
+++ b/solution.py
@@ -143,16 +143,6 @@
         pl.when(my_z >= z)(functools.partial(greet, at_blk(0, -z), column_hello.at[z - 1]))
     for y in far_rows:
         pl.when(turn_at_row(y) < row_turn)(functools.partial(greet, at_blk(y, 0), row_hello))
-    for x, core in lev_offsets:
-        pl.when(turn_at_lev(x, core) < lev_turn)(
-            functools.partial(greet, (me, at_lev(x, core)), lev_hello)
-        )
-
-    def load_op(l, carry):
-        pltpu.make_async_copy(op_hbm.at[:, l], op_v.at[l, pl.ds(0, fields)], op_sem).start()
-        return carry
-
-    lax.fori_loop(0, levs, load_op, 0)
 
     before = onehot(rows_of((width, width)) < lanes_of((width, width)))
     loads[0].wait()
@@ -250,6 +240,17 @@
     mid_a[quarter] = out_a[quarter]
     in_a[quarter, 0] = out_a[quarter, 0]
 
+    for x, core in lev_offsets:
+        pl.when(turn_at_lev(x, core) < lev_turn)(
+            functools.partial(greet, (me, at_lev(x, core)), lev_hello)
+        )
+
+    def load_op(l, carry):
+        pltpu.make_async_copy(op_hbm.at[:, l], op_v.at[l, pl.ds(0, fields)], op_sem).start()
+        return carry
+
+    lax.fori_loop(0, levs, load_op, 0)
+
     def blk_copy(src, dst, at, far, first, count, to):
         return pltpu.make_async_remote_copy(
             src_ref=src.at[pl.ds(first, count)],
@@ -260,11 +261,11 @@
             device_id_type=MESH,
         )
 
-    def blk_send(src, dst, at):
+    def blk_send(src, dst, at, far):
         for y, z in offsets:
             tile = tile_of(y, z)
-            blk_copy(src, dst, at, int(tile >= half_tiles), tile, 1, at_blk(y, z)).start()
-        dst[own_tile] = src[own_tile]
+            if tile // half_tiles == far:
+                blk_copy(src, dst, at, far, tile, 1, at_blk(y, z)).start()
 
     def blk_arrived(src, dst, at, far):
         count = half_tiles - 1 + far
@@ -394,9 +395,14 @@
     beside = jnp.concatenate(
         [jnp.where(on_side, beside, none), jnp.where(on_side, none, beside)], axis=0
     )
-    summed = partial[...] + dot_nn(step_halo[...], beside)
-    out_c[...] = (0.2 * summed).reshape(blocks, HALF, LANES).astype(BF16)
-    blk_send(out_c, in_c, 3)
+    for far in (1, 0):
+        here = pl.ds(far * half, half)
+        summed = partial[here, :] + dot_nn(step_halo[here, :], beside)
+        out_c[pl.ds(far * half_tiles, half_tiles)] = (
+            (0.2 * summed).reshape(half_tiles, HALF, LANES).astype(BF16)
+        )
+        blk_send(out_c, in_c, 3, far)
+    in_c[own_tile] = out_c[own_tile]
 
     per = levs * CAP
     line = rows_of((per, rows))

time: 50.9 us -> 50.4 us (level)
  no operation moved by 1% of the time
where the time goes in v4:
time: 50.4 us; the launch traced here: 50.3 us
  Pallas kernels  48.7 us (97%)
  local copies, waits for them, and re-layouts  1.55 us (3%)
    pallas_call x1, Pallas kernels, local(): pl.pallas_call(functools.partial(kernel, blocks, levs), out_shape=jax.Sha...  48.7 us
    unnamed x1, local copies, waits for them, and re-layouts  1.55 us

profile of v4, /device:TPU:1, one launch (start us, length us, event | category | flops | bytes accessed | tf_op | source)
XLA Modules:
  0.0 50.3 jit_solution(3161940507747595682)
XLA Ops:
  0.0 48.7 %shard_map.55 = f32[7,32,128]{2,1,0:T(8,128)} custom-call(bf16[7,8,512]{2,1,0:T(8,128)(2,1)} %io_hbm.1, s32[1,512]{1,0:T(1,128)} %bitcast.6, s32[1,512]{1,0:T(1,128)} %bitcast.7, s32[4,512]{1,0:T(4,128)} %near_hbm.1, bf16[7,16,8,896]{3,2,1,0:T(8,128)(2,1)} %bitcast.4), custom_call_target="tpu_custom_call" | custom-call | tf_op jit(solution)/shard_map/pallas_call | solution.py:491
  48.7 1.6 %copy.7 = f32[32,7,128]{2,0,1:T(8,128)} copy(f32[32,7,128]{2,0,1:T(8,128)} %bitcast.5) | data formatting | bytes 229376

commit v5 on v4

--- a/solution.py
+++ b/solution.py
@@ -139,7 +139,7 @@
         pl.when(count > 0)(functools.partial(pl.semaphore_wait, semaphore, count))
 
     hear(barrier, my_z * side_y + row_turn + lev_turn)
-    for z in range(1, side_z):
+    for z in far_columns:
         pl.when(my_z >= z)(functools.partial(greet, at_blk(0, -z), column_hello.at[z - 1]))
     for y in far_rows:
         pl.when(turn_at_row(y) < row_turn)(functools.partial(greet, at_blk(y, 0), row_hello))
@@ -274,6 +274,24 @@
     def blk_sent(src, dst, at):
         blk_copy(src, dst, at, 0, 0, blocks - 1, at_blk(0, 1)).wait_send()
 
+    def column_copy(first, count, z):
+        return pltpu.make_async_remote_copy(
+            src_ref=mid_a.at[:, pl.ds(first, count)],
+            dst_ref=in_a.at[:, pl.ds(first, count)],
+            send_sem=sems.at[0],
+            recv_sem=sems.at[1],
+            device_id=at_blk(0, z),
+            device_id_type=MESH,
+        )
+
+    for z in range(1, side_z):
+
+        @pl.when(my_z + z < side_z)
+        def _():
+            row_copy(0, side_y - 1, z, at_blk(1, 0)).wait_recv()
+            pl.semaphore_wait(column_hello.at[z - 1], 1)
+            column_copy(z, 1, z).start()
+
     loads[3].wait()
     near = (near_v[...] - me * width + HALO) & (total - 1)
     near = jnp.where(
@@ -317,24 +335,6 @@
         choose = jnp.where(here & (choose_lane == lane), 32.0, choose)
         choose = jnp.where(here & (choose_lane == lane + 1), 1.0, choose)
     choose = choose.astype(BF16)
-
-    def column_copy(first, count, z):
-        return pltpu.make_async_remote_copy(
-            src_ref=mid_a.at[:, pl.ds(first, count)],
-            dst_ref=in_a.at[:, pl.ds(first, count)],
-            send_sem=sems.at[0],
-            recv_sem=sems.at[1],
-            device_id=at_blk(0, z),
-            device_id_type=MESH,
-        )
-
-    for z in range(1, side_z):
-
-        @pl.when(my_z + z < side_z)
-        def _():
-            row_copy(0, side_y - 1, z, at_blk(1, 0)).wait_recv()
-            pl.semaphore_wait(column_hello.at[z - 1], 1)
-            column_copy(z, 1, z).start()
 
     row_tiles = pltpu.make_async_remote_copy(
         src_ref=out_a.at[pl.ds(0, side_y - 1), 0],

time: 50.4 us -> 50.4 us (level)
  no operation moved by 1% of the time
where the time goes in v5:
time: 50.4 us; the launch traced here: 50.3 us
  Pallas kernels  48.7 us (97%)
  local copies, waits for them, and re-layouts  1.55 us (3%)
    pallas_call x1, Pallas kernels, local(): pl.pallas_call(functools.partial(kernel, blocks, levs), out_shape=jax.Sha...  48.7 us
    unnamed x1, local copies, waits for them, and re-layouts  1.55 us

profile of v5, /device:TPU:1, one launch (start us, length us, event | category | flops | bytes accessed | tf_op | source)
XLA Modules:
  0.0 50.3 jit_solution(5893324128010376053)
XLA Ops:
  0.0 48.7 %shard_map.55 = f32[7,32,128]{2,1,0:T(8,128)} custom-call(bf16[7,8,512]{2,1,0:T(8,128)(2,1)} %io_hbm.1, s32[1,512]{1,0:T(1,128)} %bitcast.6, s32[1,512]{1,0:T(1,128)} %bitcast.7, s32[4,512]{1,0:T(4,128)} %near_hbm.1, bf16[7,16,8,896]{3,2,1,0:T(8,128)(2,1)} %bitcast.4), custom_call_target="tpu_custom_call" | custom-call | tf_op jit(solution)/shard_map/pallas_call | solution.py:491
  48.7 1.6 %copy.7 = f32[32,7,128]{2,0,1:T(8,128)} copy(f32[32,7,128]{2,0,1:T(8,128)} %bitcast.5) | data formatting | bytes 229376
